TPU v7x, 32 devices: a whole 2x2x4 slice. The times are simulated.
32 devices in a mesh: group: 2 (over x), tile: 16 (over z, y, core).
Axes of the slice: x: 2, y: 2, z: 4, core: 2. Of those that a mesh axis runs over, the one named last changes fastest.
Arguments:
- query_tokens: bfloat16 [6144, 1536], P(('group', 'tile')), parts along dimension 0, may hold values from -6 to 6
- key_tokens: bfloat16 [6144, 1536], P(('group', 'tile')), parts along dimension 0, may hold values from -6 to 6
- value_tokens: bfloat16 [6144, 1536], P(('group', 'tile')), parts along dimension 0, may hold values from -6 to 6
- forward_out: bfloat16 [6144, 1536], P(('group', 'tile')), parts along dimension 0, may hold values from -3 to 3
- out_grad: bfloat16 [6144, 1536], P(('group', 'tile')), parts along dimension 0, may hold values from -192 to 192
- log_norm: float32 [12, 6144], P(None, ('group', 'tile')), parts along dimension 1, may hold values from 7.5 to 9
- window_ids: int32 [12, 16, 5], P(None, 'tile'), may hold values from -1 to 15, as said below
Outputs:
- grad_queries: bfloat16 [6144, 1536], P(('group', 'tile')), parts along dimension 0
- grad_keys: bfloat16 [6144, 1536], P(('group', 'tile')), parts along dimension 0
- grad_values: bfloat16 [6144, 1536], P(('group', 'tile')), parts along dimension 0
There are 2 independent parts, one for each index of `group`. A program takes and returns all parts, laid end to end along the dimension named above; an argument that names none is the same for every part. Nothing has to cross between parts.
Inputs may be any that keep to these rules, and one draw needn't show every extreme that they name: Tiles are numbered width fastest, then height, then time, on a grid of 2 x 1 x 8. window_ids[h, i, 0] is the tile beside tile i along time; entries 1 and 2 are the tiles before and after tile i along width; entries 3 and 4 are the tiles before and after, along width, of the tile beside i along time. An entry is -1 where that tile does not exist or lies outside head h's window; each head's window has one shape, a block of tiles along time and width, clipped at the grid's border.
All inputs are finite; a program needn't handle non-finite values.
Results may differ from a plain program's by a relative error of at most 0.0075.
Values may be sent and summed in bfloat16 or wider, within the bound.
No kernel may reach another device: no remote copies, remote signals or barrier semaphores. Data moves between devices by JAX's collectives and lax.ppermute only.
A program may use at most 64 MiB of HBM per device.

v0:
```python
import math

import jax
import jax.numpy as jnp
from jax import lax
from jax.sharding import PartitionSpec as P


def passed_along(value, axis, steps):
    count = lax.axis_size(axis)
    initial, last = (max(0, -steps), min(count, count - steps))
    return lax.ppermute(value, axis, [(source, source + steps) for source in range(initial, last)])


def shortened(value):

    def short(part):
        return part.astype(jnp.bfloat16) if part.dtype == jnp.float32 else part

    return jax.tree.map(short, value)


def pair_terms(query_heads, grad_heads, log_part, delta_part, key_heads, value_heads, score_scale):
    scores = (
        jnp.einsum("thd,shd->hts", query_heads, key_heads, preferred_element_type=jnp.float32)
        * score_scale
    )
    weights = jnp.exp(scores - log_part[:, :, None])
    weights_low = weights.astype(jnp.bfloat16)
    value_term = jnp.einsum(
        "hts,thd->shd", weights_low, grad_heads, preferred_element_type=jnp.float32
    )
    grad_weights = jnp.einsum(
        "thd,shd->hts", grad_heads, value_heads, preferred_element_type=jnp.float32
    )
    grad_scores = (weights * (grad_weights - delta_part[:, :, None])).astype(jnp.bfloat16)
    query_term = (
        jnp.einsum("hts,shd->thd", grad_scores, key_heads, preferred_element_type=jnp.float32)
        * score_scale
    )
    key_term = (
        jnp.einsum("hts,thd->shd", grad_scores, query_heads, preferred_element_type=jnp.float32)
        * score_scale
    )
    return (
        query_term.astype(jnp.bfloat16),
        key_term.astype(jnp.bfloat16),
        value_term.astype(jnp.bfloat16),
    )


def body(query_tokens, key_tokens, value_tokens, forward_out, out_grad, log_norm, window_ids):
    tok_rows, features = query_tokens.shape
    head_count = log_norm.shape[0]
    head_size = features // head_count
    score_scale = 1.0 / math.sqrt(head_size)
    tile_count = lax.axis_size("tile")
    half_tiles = tile_count // 2

    def split_heads(values):
        return values.reshape(tok_rows, head_count, head_size)

    def flat(values):
        return values.reshape(tok_rows, features)

    row_delta = jnp.sum(
        split_heads(out_grad.astype(jnp.float32) * forward_out.astype(jnp.float32)), axis=2
    ).T
    key_value = (key_tokens, value_tokens)
    pieces = [
        passed_along((key_value[0], key_value[1]), "tile", stride)
        for stride in (half_tiles, -half_tiles)
    ]
    time_pair = (pieces[0][0] + pieces[1][0], pieces[0][1] + pieces[1][1])
    sources = [time_pair]
    for stride in (1, -1):
        sources.append(passed_along((key_value[0], key_value[1]), "tile", stride))
    for stride in (1, -1):
        sources.append(passed_along((time_pair[0], time_pair[1]), "tile", stride))
    present = (window_ids[:, 0, :] >= 0).astype(jnp.bfloat16)
    query_heads = split_heads(query_tokens)
    grad_heads = split_heads(out_grad)
    own_query, own_key, own_value = pair_terms(
        query_heads,
        grad_heads,
        log_norm,
        row_delta,
        split_heads(key_tokens),
        split_heads(value_tokens),
        score_scale,
    )
    query_total = own_query.astype(jnp.float32)
    outgoing = []
    for slot_index in range(5):
        remote_keys, remote_values = sources[slot_index]
        query_term, key_term, value_term = pair_terms(
            query_heads,
            grad_heads,
            log_norm,
            row_delta,
            split_heads(remote_keys),
            split_heads(remote_values),
            score_scale,
        )
        factor = present[:, slot_index][None, :, None]
        query_total = query_total + (query_term * factor).astype(jnp.float32)
        outgoing.append((flat(key_term * factor), flat(value_term * factor)))
    time_keys = outgoing[0][0].astype(jnp.float32)
    time_values = outgoing[0][1].astype(jnp.float32)
    for slot_index, stride in ((3, -1), (4, 1)):
        moved = passed_along(shortened(outgoing[slot_index]), "tile", stride)
        time_keys = time_keys + moved[0].astype(jnp.float32)
        time_values = time_values + moved[1].astype(jnp.float32)
    time_out = (time_keys.astype(jnp.bfloat16), time_values.astype(jnp.bfloat16))
    incoming = [
        passed_along((time_out[0], time_out[1]), "tile", stride)
        for stride in (half_tiles, -half_tiles)
    ]
    for slot_index, stride in ((1, -1), (2, 1)):
        incoming.append(passed_along(shortened(outgoing[slot_index]), "tile", stride))
    key_total = flat(own_key).astype(jnp.float32)
    value_total = flat(own_value).astype(jnp.float32)
    for arrived in incoming:
        key_total = key_total + arrived[0].astype(jnp.float32)
        value_total = value_total + arrived[1].astype(jnp.float32)
    return (
        flat(query_total).astype(jnp.bfloat16),
        key_total.astype(jnp.bfloat16),
        value_total.astype(jnp.bfloat16),
    )


def solution(mesh):
    placed = (
        P(("group", "tile"), None),
        P(("group", "tile"), None),
        P(("group", "tile"), None),
        P(("group", "tile"), None),
        P(("group", "tile"), None),
        P(None, ("group", "tile")),
        P(None, "tile", None),
    )
    return jax.shard_map(
        body,
        mesh=mesh,
        in_specs=placed,
        out_specs=(
            P(("group", "tile"), None),
            P(("group", "tile"), None),
            P(("group", "tile"), None),
        ),
        check_vma=False,
    )
```

profile of v0, /device:TPU:31, one launch (start us, length us, event | category | flops | bytes accessed | tf_op | source)
XLA Modules:
  0.0 202.3 jit_solution(15436066965895794647)
XLA Ops:
  0.6 2.9 %collective-permute-start.3 = (bf16[192,1536]{1,0:T(8,128)(2,1)}, bf16[192,1536]{1,0:T(8,128)(2,1)}, u32[]{:S(2)}, u32[]{:S(2)}) collective-permute-start(bf16[192,1536]{1,0:T(8,128)(2,1)} %param.9), channel_id=1, source_target_pairs={{8,0},{9,1},{10,2},{11,3},{12,4},{13,5},{14,6},{15,7},{24,16},{25,... | collective-permute-start | bytes 1769480 | tf_op jit(solution)/shard_map/ppermute | solution.py:12
  4.9 6.5 %collective-permute-start.1 = (bf16[192,1536]{1,0:T(8,128)(2,1)}, bf16[192,1536]{1,0:T(8,128)(2,1)}, u32[]{:S(2)}, u32[]{:S(2)}) collective-permute-start(bf16[192,1536]{1,0:T(8,128)(2,1)} %param.8), channel_id=1, source_target_pairs={{8,0},{9,1},{10,2},{11,3},{12,4},{13,5},{14,6},{15,7},{24,16},{25,... | collective-permute-start | bytes 1769480 | tf_op jit(solution)/shard_map/ppermute | solution.py:12
  14.7 1.4 convert_multiply_fusion
  20.2 1.5 fusion.29
  21.7 4.1 %collective-permute-start.7 = (bf16[192,1536]{1,0:T(8,128)(2,1)S(1)}, bf16[192,1536]{1,0:T(8,128)(2,1)S(1)}, u32[]{:S(2)}, u32[]{:S(2)}) collective-permute-start(bf16[192,1536]{1,0:T(8,128)(2,1)S(1)} %copy-done.4), channel_id=1, source_target_pairs={{1,0},{2,1},{3,2},{4,3},{5,4},{6,5},{7,6},{8,7},{9,8},{10,9},{11,1... | collective-permute-start | bytes 1769480 | tf_op jit(solution)/shard_map/ppermute | solution.py:12
  25.8 21.3 %collective-permute-done.2 = bf16[192,1536]{1,0:T(8,128)(2,1)} collective-permute-done((bf16[192,1536]{1,0:T(8,128)(2,1)}, bf16[192,1536]{1,0:T(8,128)(2,1)}, u32[]{:S(2)}, u32[]{:S(2)}) %collective-permute-start.2) | collective-permute-done | bytes 589856 | tf_op jit(solution)/shard_map/ppermute | solution.py:12
  48.4 1.4 add.58
  49.8 3.2 %collective-permute-start.6 = (bf16[192,1536]{1,0:T(8,128)(2,1)S(1)}, bf16[192,1536]{1,0:T(8,128)(2,1)S(1)}, u32[]{:S(2)}, u32[]{:S(2)}) collective-permute-start(bf16[192,1536]{1,0:T(8,128)(2,1)S(1)} %copy-done.2), channel_id=1, source_target_pairs={{1,0},{2,1},{3,2},{4,3},{5,4},{6,5},{7,6},{8,7},{9,8},{10,9},{11,1... | collective-permute-start | bytes 1769480 | tf_op jit(solution)/shard_map/ppermute | solution.py:12
  52.9 6.8 %collective-permute-done = bf16[192,1536]{1,0:T(8,128)(2,1)} collective-permute-done((bf16[192,1536]{1,0:T(8,128)(2,1)}, bf16[192,1536]{1,0:T(8,128)(2,1)}, u32[]{:S(2)}, u32[]{:S(2)}) %collective-permute-start) | collective-permute-done | bytes 589856 | tf_op jit(solution)/shard_map/ppermute | solution.py:12
  59.8 2.5 %collective-permute-start.11 = (bf16[192,1536]{1,0:T(8,128)(2,1)S(1)}, bf16[192,1536]{1,0:T(8,128)(2,1)S(1)}, u32[]{:S(2)}, u32[]{:S(2)}) collective-permute-start(bf16[192,1536]{1,0:T(8,128)(2,1)S(1)} %add.58), channel_id=1, source_target_pairs={{1,0},{2,1},{3,2},{4,3},{5,4},{6,5},{7,6},{8,7},{9,8},{10,9},{11,1... | collective-permute-start | bytes 1769480 | tf_op jit(solution)/shard_map/ppermute | solution.py:12
  62.3 1.4 add.57
  65.5 1.5 fusion.116
  69.4 7.1 %collective-permute-start.10 = (bf16[192,1536]{1,0:T(8,128)(2,1)S(1)}, bf16[192,1536]{1,0:T(8,128)(2,1)S(1)}, u32[]{:S(2)}, u32[]{:S(2)}) collective-permute-start(bf16[192,1536]{1,0:T(8,128)(2,1)S(1)} %add.57), channel_id=1, source_target_pairs={{1,0},{2,1},{3,2},{4,3},{5,4},{6,5},{7,6},{8,7},{9,8},{10,9},{11,1... | collective-permute-start | bytes 1769480 | tf_op jit(solution)/shard_map/ppermute | solution.py:12
  82.8 4.6 %collective-permute-start.22 = (bf16[192,1536]{1,0:T(8,128)(2,1)S(1)}, bf16[192,1536]{1,0:T(8,128)(2,1)S(1)}, u32[]{:S(2)}, u32[]{:S(2)}) collective-permute-start(bf16[192,1536]{1,0:T(8,128)(2,1)S(1)} %bitcast.389), channel_id=1, source_target_pairs={{1,0},{2,1},{3,2},{4,3},{5,4},{6,5},{7,6},{8,7},{9,8},{10,9},{11,1... | collective-permute-start | bytes 1769480 | tf_op jit(solution)/shard_map/ppermute | solution.py:12
  89.1 1.5 fusion.48
  94.8 4.3 %collective-permute-start.12 = (bf16[192,1536]{1,0:T(8,128)(2,1)S(1)}, bf16[192,1536]{1,0:T(8,128)(2,1)S(1)}, u32[]{:S(2)}, u32[]{:S(2)}) collective-permute-start(bf16[192,1536]{1,0:T(8,128)(2,1)S(1)} %bitcast.390), channel_id=1, source_target_pairs={{1,0},{2,1},{3,2},{4,3},{5,4},{6,5},{7,6},{8,7},{9,8},{10,9},{11,1... | collective-permute-start | bytes 1769480 | tf_op jit(solution)/shard_map/ppermute | solution.py:12
  99.1 3.6 %collective-permute-start.18 = (bf16[192,1536]{1,0:T(8,128)(2,1)S(1)}, bf16[192,1536]{1,0:T(8,128)(2,1)S(1)}, u32[]{:S(2)}, u32[]{:S(2)}) collective-permute-start(bf16[192,1536]{1,0:T(8,128)(2,1)S(1)} %bitcast.391), channel_id=1, source_target_pairs={{1,0},{2,1},{3,2},{4,3},{5,4},{6,5},{7,6},{8,7},{9,8},{10,9},{11,1... | collective-permute-start | bytes 1769480 | tf_op jit(solution)/shard_map/ppermute | solution.py:12
  108.4 3.8 %collective-permute-done.19 = bf16[192,1536]{1,0:T(8,128)(2,1)S(1)} collective-permute-done((bf16[192,1536]{1,0:T(8,128)(2,1)S(1)}, bf16[192,1536]{1,0:T(8,128)(2,1)S(1)}, u32[]{:S(2)}, u32[]{:S(2)}) %collective-permute-start.19) | collective-permute-done | bytes 589856 | tf_op jit(solution)/shard_map/ppermute | solution.py:12
  112.4 18.1 %collective-permute-start.21 = (bf16[192,1536]{1,0:T(8,128)(2,1)S(1)}, bf16[192,1536]{1,0:T(8,128)(2,1)S(1)}, u32[]{:S(2)}, u32[]{:S(2)}) collective-permute-start(bf16[192,1536]{1,0:T(8,128)(2,1)S(1)} %fusion.75), channel_id=1, source_target_pairs={{8,0},{9,1},{10,2},{11,3},{12,4},{13,5},{14,6},{15,7},{24,16},{25,... | collective-permute-start | bytes 1769480 | tf_op jit(solution)/shard_map/ppermute | solution.py:12
  131.2 4.8 %collective-permute-start.16 = (bf16[192,1536]{1,0:T(8,128)(2,1)S(1)}, bf16[192,1536]{1,0:T(8,128)(2,1)S(1)}, u32[]{:S(2)}, u32[]{:S(2)}) collective-permute-start(bf16[192,1536]{1,0:T(8,128)(2,1)S(1)} %bitcast.386), channel_id=1, source_target_pairs={{1,0},{2,1},{3,2},{4,3},{5,4},{6,5},{7,6},{8,7},{9,8},{10,9},{11,1... | collective-permute-start | bytes 1769480 | tf_op jit(solution)/shard_map/ppermute | solution.py:12
  137.6 1.3 collective-permute-start.17
  138.9 15.8 %collective-permute-start.15 = (bf16[192,1536]{1,0:T(8,128)(2,1)S(1)}, bf16[192,1536]{1,0:T(8,128)(2,1)S(1)}, u32[]{:S(2)}, u32[]{:S(2)}) collective-permute-start(bf16[192,1536]{1,0:T(8,128)(2,1)S(1)} %fusion.81), channel_id=1, source_target_pairs={{8,0},{9,1},{10,2},{11,3},{12,4},{13,5},{14,6},{15,7},{24,16},{25,... | collective-permute-start | bytes 1769480 | tf_op jit(solution)/shard_map/ppermute | solution.py:12
  158.6 8.7 %collective-permute-done.15 = bf16[192,1536]{1,0:T(8,128)(2,1)S(1)} collective-permute-done((bf16[192,1536]{1,0:T(8,128)(2,1)S(1)}, bf16[192,1536]{1,0:T(8,128)(2,1)S(1)}, u32[]{:S(2)}, u32[]{:S(2)}) %collective-permute-start.15) | collective-permute-done | bytes 589856 | tf_op jit(solution)/shard_map/ppermute | solution.py:12
  167.3 33.9 %collective-permute-done.14 = bf16[192,1536]{1,0:T(8,128)(2,1)S(1)} collective-permute-done((bf16[192,1536]{1,0:T(8,128)(2,1)S(1)}, bf16[192,1536]{1,0:T(8,128)(2,1)S(1)}, u32[]{:S(2)}, u32[]{:S(2)}) %collective-permute-start.14) | collective-permute-done | bytes 589856 | tf_op jit(solution)/shard_map/ppermute | solution.py:12
  (85 shorter events, 39.1 us)
Async XLA Ops:
  0.6 21.0 %collective-permute-start.3 = (bf16[192,1536]{1,0:T(8,128)(2,1)}, bf16[192,1536]{1,0:T(8,128)(2,1)}, u32[]{:S(2)}, u32[]{:S(2)}) collective-permute-start(bf16[192,1536]{1,0:T(8,128)(2,1)} %param.9), channel_id=1, source_target_pairs={{8,0},{9,1},{10,2},{11,3},{12,4},{13,5},{14,6},{15,7},{24,16},{25,... | collective-permute-start | bytes 1769480 | tf_op jit(solution)/shard_map/ppermute | solution.py:12
  3.6 43.5 %collective-permute-start.2 = (bf16[192,1536]{1,0:T(8,128)(2,1)}, bf16[192,1536]{1,0:T(8,128)(2,1)}, u32[]{:S(2)}, u32[]{:S(2)}) collective-permute-start(bf16[192,1536]{1,0:T(8,128)(2,1)} %param.9), channel_id=1, source_target_pairs={{0,8},{1,9},{2,10},{3,11},{4,12},{5,13},{6,14},{7,15},{16,24},{17,... | collective-permute-start | bytes 1769480 | tf_op jit(solution)/shard_map/ppermute | solution.py:12
  4.9 44.9 %collective-permute-start.1 = (bf16[192,1536]{1,0:T(8,128)(2,1)}, bf16[192,1536]{1,0:T(8,128)(2,1)}, u32[]{:S(2)}, u32[]{:S(2)}) collective-permute-start(bf16[192,1536]{1,0:T(8,128)(2,1)} %param.8), channel_id=1, source_target_pairs={{8,0},{9,1},{10,2},{11,3},{12,4},{13,5},{14,6},{15,7},{24,16},{25,... | collective-permute-start | bytes 1769480 | tf_op jit(solution)/shard_map/ppermute | solution.py:12
  11.4 48.4 %collective-permute-start = (bf16[192,1536]{1,0:T(8,128)(2,1)}, bf16[192,1536]{1,0:T(8,128)(2,1)}, u32[]{:S(2)}, u32[]{:S(2)}) collective-permute-start(bf16[192,1536]{1,0:T(8,128)(2,1)} %param.8), channel_id=1, source_target_pairs={{0,8},{1,9},{2,10},{3,11},{4,12},{5,13},{6,14},{7,15},{16,24},{17,... | collective-permute-start | bytes 1769480 | tf_op jit(solution)/shard_map/ppermute | solution.py:12
  12.7 51.5 %collective-permute-start.4 = (bf16[192,1536]{1,0:T(8,128)(2,1)}, bf16[192,1536]{1,0:T(8,128)(2,1)}, u32[]{:S(2)}, u32[]{:S(2)}) collective-permute-start(bf16[192,1536]{1,0:T(8,128)(2,1)} %param.8), channel_id=1, source_target_pairs={{0,1},{1,2},{2,3},{3,4},{4,5},{5,6},{6,7},{7,8},{8,9},{9,10},{10,1... | collective-permute-start | bytes 1769480 | tf_op jit(solution)/shard_map/ppermute | solution.py:12
  21.7 61.1 %collective-permute-start.7 = (bf16[192,1536]{1,0:T(8,128)(2,1)S(1)}, bf16[192,1536]{1,0:T(8,128)(2,1)S(1)}, u32[]{:S(2)}, u32[]{:S(2)}) collective-permute-start(bf16[192,1536]{1,0:T(8,128)(2,1)S(1)} %copy-done.4), channel_id=1, source_target_pairs={{1,0},{2,1},{3,2},{4,3},{5,4},{6,5},{7,6},{8,7},{9,8},{10,9},{11,1... | collective-permute-start | bytes 1769480 | tf_op jit(solution)/shard_map/ppermute | solution.py:12
  47.1 31.2 %collective-permute-start.5 = (bf16[192,1536]{1,0:T(8,128)(2,1)S(1)}, bf16[192,1536]{1,0:T(8,128)(2,1)S(1)}, u32[]{:S(2)}, u32[]{:S(2)}) collective-permute-start(bf16[192,1536]{1,0:T(8,128)(2,1)S(1)} %copy-done.4), channel_id=1, source_target_pairs={{0,1},{1,2},{2,3},{3,4},{4,5},{5,6},{6,7},{7,8},{8,9},{9,10},{10,1... | collective-permute-start | bytes 1769480 | tf_op jit(solution)/shard_map/ppermute | solution.py:12
  49.8 19.6 %collective-permute-start.6 = (bf16[192,1536]{1,0:T(8,128)(2,1)S(1)}, bf16[192,1536]{1,0:T(8,128)(2,1)S(1)}, u32[]{:S(2)}, u32[]{:S(2)}) collective-permute-start(bf16[192,1536]{1,0:T(8,128)(2,1)S(1)} %copy-done.2), channel_id=1, source_target_pairs={{1,0},{2,1},{3,2},{4,3},{5,4},{6,5},{7,6},{8,7},{9,8},{10,9},{11,1... | collective-permute-start | bytes 1769480 | tf_op jit(solution)/shard_map/ppermute | solution.py:12
  59.8 44.1 %collective-permute-start.11 = (bf16[192,1536]{1,0:T(8,128)(2,1)S(1)}, bf16[192,1536]{1,0:T(8,128)(2,1)S(1)}, u32[]{:S(2)}, u32[]{:S(2)}) collective-permute-start(bf16[192,1536]{1,0:T(8,128)(2,1)S(1)} %add.58), channel_id=1, source_target_pairs={{1,0},{2,1},{3,2},{4,3},{5,4},{6,5},{7,6},{8,7},{9,8},{10,9},{11,1... | collective-permute-start | bytes 1769480 | tf_op jit(solution)/shard_map/ppermute | solution.py:12
  64.2 29.3 %collective-permute-start.9 = (bf16[192,1536]{1,0:T(8,128)(2,1)S(1)}, bf16[192,1536]{1,0:T(8,128)(2,1)S(1)}, u32[]{:S(2)}, u32[]{:S(2)}) collective-permute-start(bf16[192,1536]{1,0:T(8,128)(2,1)S(1)} %add.58), channel_id=1, source_target_pairs={{0,1},{1,2},{2,3},{3,4},{4,5},{5,6},{6,7},{7,8},{8,9},{9,10},{10,1... | collective-permute-start | bytes 1769480 | tf_op jit(solution)/shard_map/ppermute | solution.py:12
  69.4 29.6 %collective-permute-start.10 = (bf16[192,1536]{1,0:T(8,128)(2,1)S(1)}, bf16[192,1536]{1,0:T(8,128)(2,1)S(1)}, u32[]{:S(2)}, u32[]{:S(2)}) collective-permute-start(bf16[192,1536]{1,0:T(8,128)(2,1)S(1)} %add.57), channel_id=1, source_target_pairs={{1,0},{2,1},{3,2},{4,3},{5,4},{6,5},{7,6},{8,7},{9,8},{10,9},{11,1... | collective-permute-start | bytes 1769480 | tf_op jit(solution)/shard_map/ppermute | solution.py:12
  78.3 12.8 %collective-permute-start.8 = (bf16[192,1536]{1,0:T(8,128)(2,1)S(1)}, bf16[192,1536]{1,0:T(8,128)(2,1)S(1)}, u32[]{:S(2)}, u32[]{:S(2)}) collective-permute-start(bf16[192,1536]{1,0:T(8,128)(2,1)S(1)} %add.57), channel_id=1, source_target_pairs={{0,1},{1,2},{2,3},{3,4},{4,5},{5,6},{6,7},{7,8},{8,9},{9,10},{10,1... | collective-permute-start | bytes 1769480 | tf_op jit(solution)/shard_map/ppermute | solution.py:12
  82.8 54.8 %collective-permute-start.22 = (bf16[192,1536]{1,0:T(8,128)(2,1)S(1)}, bf16[192,1536]{1,0:T(8,128)(2,1)S(1)}, u32[]{:S(2)}, u32[]{:S(2)}) collective-permute-start(bf16[192,1536]{1,0:T(8,128)(2,1)S(1)} %bitcast.389), channel_id=1, source_target_pairs={{1,0},{2,1},{3,2},{4,3},{5,4},{6,5},{7,6},{8,7},{9,8},{10,9},{11,1... | collective-permute-start | bytes 1769480 | tf_op jit(solution)/shard_map/ppermute | solution.py:12
  91.1 47.8 %collective-permute-start.23 = (bf16[192,1536]{1,0:T(8,128)(2,1)S(1)}, bf16[192,1536]{1,0:T(8,128)(2,1)S(1)}, u32[]{:S(2)}, u32[]{:S(2)}) collective-permute-start(bf16[192,1536]{1,0:T(8,128)(2,1)S(1)} %bitcast.388), channel_id=1, source_target_pairs={{0,1},{1,2},{2,3},{3,4},{4,5},{5,6},{6,7},{7,8},{8,9},{9,10},{10,1... | collective-permute-start | bytes 1769480 | tf_op jit(solution)/shard_map/ppermute | solution.py:12
  94.8 36.4 %collective-permute-start.12 = (bf16[192,1536]{1,0:T(8,128)(2,1)S(1)}, bf16[192,1536]{1,0:T(8,128)(2,1)S(1)}, u32[]{:S(2)}, u32[]{:S(2)}) collective-permute-start(bf16[192,1536]{1,0:T(8,128)(2,1)S(1)} %bitcast.390), channel_id=1, source_target_pairs={{1,0},{2,1},{3,2},{4,3},{5,4},{6,5},{7,6},{8,7},{9,8},{10,9},{11,1... | collective-permute-start | bytes 1769480 | tf_op jit(solution)/shard_map/ppermute | solution.py:12
  99.1 8.0 %collective-permute-start.18 = (bf16[192,1536]{1,0:T(8,128)(2,1)S(1)}, bf16[192,1536]{1,0:T(8,128)(2,1)S(1)}, u32[]{:S(2)}, u32[]{:S(2)}) collective-permute-start(bf16[192,1536]{1,0:T(8,128)(2,1)S(1)} %bitcast.391), channel_id=1, source_target_pairs={{1,0},{2,1},{3,2},{4,3},{5,4},{6,5},{7,6},{8,7},{9,8},{10,9},{11,1... | collective-permute-start | bytes 1769480 | tf_op jit(solution)/shard_map/ppermute | solution.py:12
  103.8 8.4 %collective-permute-start.19 = (bf16[192,1536]{1,0:T(8,128)(2,1)S(1)}, bf16[192,1536]{1,0:T(8,128)(2,1)S(1)}, u32[]{:S(2)}, u32[]{:S(2)}) collective-permute-start(bf16[192,1536]{1,0:T(8,128)(2,1)S(1)} %bitcast.394), channel_id=1, source_target_pairs={{0,1},{1,2},{2,3},{3,4},{4,5},{5,6},{6,7},{7,8},{8,9},{9,10},{10,1... | collective-permute-start | bytes 1769480 | tf_op jit(solution)/shard_map/ppermute | solution.py:12
  107.1 28.9 %collective-permute-start.13 = (bf16[192,1536]{1,0:T(8,128)(2,1)S(1)}, bf16[192,1536]{1,0:T(8,128)(2,1)S(1)}, u32[]{:S(2)}, u32[]{:S(2)}) collective-permute-start(bf16[192,1536]{1,0:T(8,128)(2,1)S(1)} %bitcast.393), channel_id=1, source_target_pairs={{0,1},{1,2},{2,3},{3,4},{4,5},{5,6},{6,7},{7,8},{8,9},{9,10},{10,1... | collective-permute-start | bytes 1769480 | tf_op jit(solution)/shard_map/ppermute | solution.py:12
  112.4 42.3 %collective-permute-start.21 = (bf16[192,1536]{1,0:T(8,128)(2,1)S(1)}, bf16[192,1536]{1,0:T(8,128)(2,1)S(1)}, u32[]{:S(2)}, u32[]{:S(2)}) collective-permute-start(bf16[192,1536]{1,0:T(8,128)(2,1)S(1)} %fusion.75), channel_id=1, source_target_pairs={{8,0},{9,1},{10,2},{11,3},{12,4},{13,5},{14,6},{15,7},{24,16},{25,... | collective-permute-start | bytes 1769480 | tf_op jit(solution)/shard_map/ppermute | solution.py:12
  131.2 27.4 %collective-permute-start.16 = (bf16[192,1536]{1,0:T(8,128)(2,1)S(1)}, bf16[192,1536]{1,0:T(8,128)(2,1)S(1)}, u32[]{:S(2)}, u32[]{:S(2)}) collective-permute-start(bf16[192,1536]{1,0:T(8,128)(2,1)S(1)} %bitcast.386), channel_id=1, source_target_pairs={{1,0},{2,1},{3,2},{4,3},{5,4},{6,5},{7,6},{8,7},{9,8},{10,9},{11,1... | collective-permute-start | bytes 1769480 | tf_op jit(solution)/shard_map/ppermute | solution.py:12
  136.0 21.4 %collective-permute-start.20 = (bf16[192,1536]{1,0:T(8,128)(2,1)S(1)}, bf16[192,1536]{1,0:T(8,128)(2,1)S(1)}, u32[]{:S(2)}, u32[]{:S(2)}) collective-permute-start(bf16[192,1536]{1,0:T(8,128)(2,1)S(1)} %fusion.75), channel_id=1, source_target_pairs={{0,8},{1,9},{2,10},{3,11},{4,12},{5,13},{6,14},{7,15},{16,24},{17,... | collective-permute-start | bytes 1769480 | tf_op jit(solution)/shard_map/ppermute | solution.py:12
  137.6 21.0 %collective-permute-start.17 = (bf16[192,1536]{1,0:T(8,128)(2,1)S(1)}, bf16[192,1536]{1,0:T(8,128)(2,1)S(1)}, u32[]{:S(2)}, u32[]{:S(2)}) collective-permute-start(bf16[192,1536]{1,0:T(8,128)(2,1)S(1)} %bitcast.387), channel_id=1, source_target_pairs={{0,1},{1,2},{2,3},{3,4},{4,5},{5,6},{6,7},{7,8},{8,9},{9,10},{10,1... | collective-permute-start | bytes 1769480 | tf_op jit(solution)/shard_map/ppermute | solution.py:12
  138.9 28.4 %collective-permute-start.15 = (bf16[192,1536]{1,0:T(8,128)(2,1)S(1)}, bf16[192,1536]{1,0:T(8,128)(2,1)S(1)}, u32[]{:S(2)}, u32[]{:S(2)}) collective-permute-start(bf16[192,1536]{1,0:T(8,128)(2,1)S(1)} %fusion.81), channel_id=1, source_target_pairs={{8,0},{9,1},{10,2},{11,3},{12,4},{13,5},{14,6},{15,7},{24,16},{25,... | collective-permute-start | bytes 1769480 | tf_op jit(solution)/shard_map/ppermute | solution.py:12
  154.7 46.5 %collective-permute-start.14 = (bf16[192,1536]{1,0:T(8,128)(2,1)S(1)}, bf16[192,1536]{1,0:T(8,128)(2,1)S(1)}, u32[]{:S(2)}, u32[]{:S(2)}) collective-permute-start(bf16[192,1536]{1,0:T(8,128)(2,1)S(1)} %fusion.81), channel_id=1, source_target_pairs={{0,8},{1,9},{2,10},{3,11},{4,12},{5,13},{6,14},{7,15},{16,24},{17,... | collective-permute-start | bytes 1769480 | tf_op jit(solution)/shard_map/ppermute | solution.py:12
  (5 other events, 20.7 us)
where the time goes:
time: 203 us; the launch traced here: 202 us
  starting transfers between devices  92.9 us (46%)
  waiting for transfers between devices  74.6 us (37%)
  matrix products  22.2 us (11%)
  other arithmetic  8.02 us (4%)
  local copies, waits for them, and re-layouts  3.32 us (2%)
    ppermute x24, starting transfers between devices, passed_along(): lax.ppermute(value, axis, [(source, source + steps) for source in range(i...  92.9 us
    ppermute x24, waiting for transfers between devices, passed_along(): lax.ppermute(value, axis, [(source, source + steps) for source in range(i...  74.6 us
    dot_general x6, matrix products, pair_terms(): jnp.einsum('hts,thd->shd', weights_low, grad_heads, preferred_element_typ...  5.6 us
    dot_general x6, matrix products, pair_terms(): jnp.einsum('thd,shd->hts', grad_heads, value_heads, preferred_element_typ...  4.76 us
    dot_general x6, matrix products, pair_terms(): jnp.einsum('hts,shd->thd', grad_scores, key_heads, preferred_element_type...  4.58 us
  transfers between devices with their start and end apart: 24, of which 5 were waited for; matrix products, arithmetic and copies ran while one was open for 15% of the time, Pallas kernels for 0%

commit v1 on v0

v1 whole, which is shorter than its diff:
```python
import functools
import math

import jax
import jax.numpy as jnp
from jax import lax
from jax.experimental import pallas as pl
from jax.experimental.pallas import tpu as pltpu
from jax.sharding import PartitionSpec as P

GRID_WIDTH = 8
ABSENT = 1e30
LOG2E = 1.4426950408889634
NT = (((1,), (1,)), ((), ()))
TN = (((0,), (0,)), ((), ()))
VMEM_LIMIT = 32 * 2**20


def dot(a, b, dims=(((1,), (0,)), ((), ()))):
    return lax.dot_general(a, b, dims, preferred_element_type=jnp.float32)


def pack_kernel(order, window, query, grad, out, log_norm, *refs, sizes):
    chunks, own_aux, send_aux = refs[: len(sizes)], refs[-2], refs[-1]
    rows = query.shape[0]
    size = query.shape[1] // log_norm.shape[0]
    ones = jnp.ones((8, size), jnp.bfloat16)
    lane = lax.broadcasted_iota(jnp.int32, (1, own_aux.shape[2] - rows), 1)

    def flag_row(head, slots):
        row = jnp.zeros(lane.shape, jnp.float32)
        for place, slot in enumerate(slots):
            if slot is not None:
                gone = jnp.where(window[head, slot] < 0, ABSENT, 0.0)
                row = jnp.where(lane == place, gone, row)
        return row

    place = 0
    for chunk, count in zip(chunks, sizes):
        for i in range(count):
            head = order[place]
            columns = pl.ds(pl.multiple_of(head * size, size), size)
            grads = grad[:, columns]
            chunk[i, 0] = query[:, columns]
            chunk[i, 1] = grads
            product = grads.astype(jnp.float32) * out[:, columns].astype(jnp.float32)
            high = product.astype(jnp.bfloat16)
            low = (product - high.astype(jnp.float32)).astype(jnp.bfloat16)
            delta = dot(ones, high, NT) + dot(ones, low, NT)
            norm = log_norm[pl.ds(head, 1), :] * LOG2E
            for aux, slots in ((own_aux, (None, 1, 2)), (send_aux, (0, 3, 4))):
                aux[place, 0:1, :rows] = norm
                aux[place, 1:2, :rows] = delta[0:1]
                aux[place, 0:1, rows:] = flag_row(head, slots)
                aux[place, 1:2, rows:] = jnp.zeros(lane.shape, jnp.float32)
            place += 1


def pack(order, window, query, grad, out, log_norm, sizes):
    rows = query.shape[0]
    heads = log_norm.shape[0]
    size = query.shape[1] // heads
    lanes = -(-(rows + 3) // 128) * 128
    whole = pl.BlockSpec(memory_space=pltpu.VMEM)
    scalar = pl.BlockSpec(memory_space=pltpu.SMEM)
    aux = jax.ShapeDtypeStruct((heads, 2, lanes), jnp.float32)
    return pl.pallas_call(
        functools.partial(pack_kernel, sizes=sizes),
        out_shape=[jax.ShapeDtypeStruct((n, 2, rows, size), jnp.bfloat16) for n in sizes] + [aux, aux],
        in_specs=[scalar, scalar] + [whole] * 4,
        out_specs=[whole] * (len(sizes) + 2),
        compiler_params=pltpu.CompilerParams(vmem_limit_bytes=VMEM_LIMIT),
        name="pack",
    )(order, window, query, grad, out, log_norm)


def terms_kernel(order, own, own_aux, other, other_aux, *refs, base, score_scale):
    keys, values, outs = refs[0:3], refs[3:6], refs[6:]
    own_query, other_query, key_values = outs[0], outs[1], outs[2:]
    rows = own.shape[2]
    place = base + pl.program_id(0)
    mine, theirs = own_aux[place], other_aux[place]
    queries = jnp.concatenate([own[0, 0], other[0, 0]], axis=0)
    grads = jnp.concatenate([own[0, 1], other[0, 1]], axis=0)
    delta = jnp.concatenate([mine[1:2, :rows], theirs[1:2, :rows]], axis=1)
    query_total = jnp.zeros(queries.shape, jnp.float32)
    for j in range(3):
        key, value = keys[j][...], values[j][...]
        norm = jnp.concatenate(
            [part[0:1, :rows] + part[0:1, rows + j : rows + j + 1] for part in (mine, theirs)], axis=1
        )
        scores = dot(key, queries, NT)
        weights = jnp.exp2(scores * (score_scale * LOG2E) - norm)
        value_term = dot(weights.astype(jnp.bfloat16), grads)
        grad_weights = dot(value, grads, NT)
        grad_scores = (weights * (grad_weights - delta)).astype(jnp.bfloat16)
        key_term = dot(grad_scores, queries) * score_scale
        query_total = query_total + dot(grad_scores, key, TN)
        key_values[j][0, 0] = key_term.astype(jnp.bfloat16)
        key_values[j][0, 1] = value_term.astype(jnp.bfloat16)
    query_total = (query_total * score_scale).astype(jnp.bfloat16)
    own_query[0] = query_total[:rows]
    other_query[0] = query_total[rows:]


def terms(order, own, own_aux, other, other_aux, keys, values, base):
    count, _, rows, size = own.shape
    score_scale = 1.0 / math.sqrt(size)
    whole = pl.BlockSpec(memory_space=pltpu.VMEM)
    packed = pl.BlockSpec((1, 2, rows, size), lambda i, order: (i, 0, 0, 0))
    one = pl.BlockSpec((1, rows, size), lambda i, order: (i, 0, 0))
    column = pl.BlockSpec((rows, size), lambda i, order: (0, order[base + i]))
    pair = jax.ShapeDtypeStruct((count, 2, rows, size), jnp.bfloat16)
    single = jax.ShapeDtypeStruct((count, rows, size), jnp.bfloat16)
    flops = count * 5 * 2 * 6 * rows * rows * size
    return pl.pallas_call(
        functools.partial(terms_kernel, base=base, score_scale=score_scale),
        out_shape=[single, single, pair, pair, pair],
        grid_spec=pltpu.PrefetchScalarGridSpec(
            num_scalar_prefetch=1,
            grid=(count,),
            in_specs=[packed, whole, packed, whole] + [column] * 6,
            out_specs=[one, one, packed, packed, packed],
        ),
        compiler_params=pltpu.CompilerParams(vmem_limit_bytes=VMEM_LIMIT),
        cost_estimate=pl.CostEstimate(
            flops=flops, bytes_accessed=count * 18 * rows * size * 2, transcendentals=count * 6 * rows * rows
        ),
        name="terms",
    )(order, own, own_aux, other, other_aux, *keys, *values)


def finish_kernel(order, *refs, sizes):
    n = len(sizes)
    own_query, back_query, own, left, right = (refs[k * n : (k + 1) * n] for k in range(5))
    query_out, key_out, value_out = refs[5 * n :]
    size = own_query[0].shape[2]
    place = 0
    for c, count in enumerate(sizes):
        for i in range(count):
            columns = pl.ds(pl.multiple_of(order[place] * size, size), size)
            query = own_query[c][i].astype(jnp.float32) + back_query[c][i].astype(jnp.float32)
            query_out[:, columns] = query.astype(jnp.bfloat16)
            for k, result in ((0, key_out), (1, value_out)):
                total = (
                    own[c][i, k].astype(jnp.float32)
                    + left[c][i, k].astype(jnp.float32)
                    + right[c][i, k].astype(jnp.float32)
                )
                result[:, columns] = total.astype(jnp.bfloat16)
            place += 1


def finish(order, parts, sizes, rows, features):
    whole = pl.BlockSpec(memory_space=pltpu.VMEM)
    result = jax.ShapeDtypeStruct((rows, features), jnp.bfloat16)
    return pl.pallas_call(
        functools.partial(finish_kernel, sizes=sizes),
        out_shape=[result] * 3,
        in_specs=[pl.BlockSpec(memory_space=pltpu.SMEM)] + [whole] * (5 * len(sizes)),
        out_specs=[whole] * 3,
        compiler_params=pltpu.CompilerParams(vmem_limit_bytes=VMEM_LIMIT),
        name="finish",
    )(order, *(part for kind in parts for part in kind))


def body(query_tokens, key_tokens, value_tokens, forward_out, out_grad, log_norm, window_ids):
    rows, features = query_tokens.shape
    heads = log_norm.shape[0]
    tiles = lax.axis_size("tile")
    beside = [(i, (i + tiles // 2) % tiles) for i in range(tiles)]
    up = [(i, i + 1) for i in range(tiles - 1) if (i + 1) % GRID_WIDTH]
    down = [(b, a) for a, b in up]
    move = lambda value, pairs: lax.ppermute(value, "tile", pairs)
    sizes = (2,) * (heads // 2)
    order = jnp.arange(heads, dtype=jnp.int32)
    *own, own_aux, send_aux = pack(order, window_ids[:, 0, :], query_tokens, out_grad, forward_out, log_norm, sizes)
    other_aux = move(send_aux, beside)
    other = [move(chunk, beside) for chunk in own]
    keys = (key_tokens, move(key_tokens, up), move(key_tokens, down))
    values = (value_tokens, move(value_tokens, up), move(value_tokens, down))
    parts = [[] for _ in range(5)]
    base = 0
    for c, count in enumerate(sizes):
        own_query, other_query, own_pair, left_pair, right_pair = terms(
            order, own[c], own_aux, other[c], other_aux, keys, values, base
        )
        made = (own_query, move(other_query, beside), own_pair, move(right_pair, up), move(left_pair, down))
        for part, value in zip(parts, made):
            part.append(value)
        base += count
    return tuple(finish(order, parts, sizes, rows, features))


def solution(mesh):
    placed = (
        P(("group", "tile"), None),
        P(("group", "tile"), None),
        P(("group", "tile"), None),
        P(("group", "tile"), None),
        P(("group", "tile"), None),
        P(None, ("group", "tile")),
        P(None, "tile", None),
    )
    return jax.shard_map(
        body,
        mesh=mesh,
        in_specs=placed,
        out_specs=(
            P(("group", "tile"), None),
            P(("group", "tile"), None),
            P(("group", "tile"), None),
        ),
        check_vma=False,
    )
```

time: 203 us -> 142 us (0.70)
  the two profiles are of different devices: /device:TPU:31 before, /device:TPU:5 now
where the time goes in v1:
time: 142 us
  starting transfers between devices  66.4 us (47%)
  waiting for transfers between devices  42.6 us (30%)
  Pallas kernels  26.9 us (19%)
  local copies, waits for them, and re-layouts  4.71 us (3%)
    ppermute x29, starting transfers between devices, body(): move = lambda value, pairs: lax.ppermute(value, 'tile', pairs)  66.4 us
    ppermute x29, waiting for transfers between devices, body(): move = lambda value, pairs: lax.ppermute(value, 'tile', pairs)  42.6 us
    pallas_call x6, Pallas kernels, terms(): pl.pallas_call(functools.partial(terms_kernel, base=base, score_scale=sco...  23.1 us
    unnamed x12, local copies, waits for them, and re-layouts  3.92 us
  transfers between devices with their start and end apart: 29, of which 6 were waited for; matrix products, arithmetic and copies ran while one was open for 1% of the time, Pallas kernels for 17%

profile of v1, /device:TPU:5, one launch (start us, length us, event | category | flops | bytes accessed | tf_op | source)
XLA Modules:
  0.0 141.5 jit_solution(17549892575719969572)
XLA Ops:
  0.6 3.7 %collective-permute-start.2 = (bf16[192,1536]{1,0:T(8,128)(2,1)}, bf16[192,1536]{1,0:T(8,128)(2,1)S(1)}, u32[]{:S(2)}, u32[]{:S(2)}) collective-permute-start(bf16[192,1536]{1,0:T(8,128)(2,1)} %refs_0_.11), channel_id=1, source_target_pairs={{0,1},{1,2},{2,3},{3,4},{4,5},{5,6},{6,7},{8,9},{9,10},{10,11},{11... | collective-permute-start | bytes 1769480 | tf_op jit(solution)/shard_map/ppermute | solution.py:174
  4.3 1.9 %collective-permute-start.3 = (bf16[192,1536]{1,0:T(8,128)(2,1)}, bf16[192,1536]{1,0:T(8,128)(2,1)S(1)}, u32[]{:S(2)}, u32[]{:S(2)}) collective-permute-start(bf16[192,1536]{1,0:T(8,128)(2,1)} %refs_0_.11), channel_id=1, source_target_pairs={{1,0},{2,1},{3,2},{4,3},{5,4},{6,5},{7,6},{9,8},{10,9},{11,10},{12... | collective-permute-start | bytes 1769480 | tf_op jit(solution)/shard_map/ppermute | solution.py:174
  6.3 4.5 %collective-permute-start.4 = (bf16[192,1536]{1,0:T(8,128)(2,1)}, bf16[192,1536]{1,0:T(8,128)(2,1)S(1)}, u32[]{:S(2)}, u32[]{:S(2)}) collective-permute-start(bf16[192,1536]{1,0:T(8,128)(2,1)} %refs_3_.11), channel_id=1, source_target_pairs={{0,1},{1,2},{2,3},{3,4},{4,5},{5,6},{6,7},{8,9},{9,10},{10,11},{11... | collective-permute-start | bytes 1769480 | tf_op jit(solution)/shard_map/ppermute | solution.py:174
  18.9 2.4 %collective-permute-start.1 = (f32[12,2,256]{2,1,0:T(2,128)S(1)}, f32[12,2,256]{2,1,0:T(2,128)S(1)}, u32[]{:S(2)}, u32[]{:S(2)}) collective-permute-start(f32[12,2,256]{2,1,0:T(2,128)S(1)} %get-tuple-element.43), channel_id=1, source_target_pairs={{0,8},{1,9},{2,10},{3,11},{4,12},{5,13},{6,14},{7,15},{8,0},{9,1},... | collective-permute-start | bytes 73736 | tf_op jit(solution)/shard_map/ppermute | solution.py:174
  22.9 2.3 %collective-permute-start.9 = (bf16[2,2,192,128]{3,2,1,0:T(8,128)(2,1)S(1)}, bf16[2,2,192,128]{3,2,1,0:T(8,128)(2,1)S(1)}, u32[]{:S(2)}, u32[]{:S(2)}) collective-permute-start(bf16[2,2,192,128]{3,2,1,0:T(8,128)(2,1)S(1)} %get-tuple-element.51.own), channel_id=1, source_target_pairs={{0,8},{1,9},{2,10},{3,11},{4,12},{5,13},{6,14},{7,15},{8,0},{9,1},... | collective-permute-start | bytes 589832 | tf_op jit(solution)/shard_map/ppermute | solution.py:174
  25.2 30.2 %collective-permute-done.9.other = bf16[2,2,192,128]{3,2,1,0:T(8,128)(2,1)S(1)} collective-permute-done((bf16[2,2,192,128]{3,2,1,0:T(8,128)(2,1)S(1)}, bf16[2,2,192,128]{3,2,1,0:T(8,128)(2,1)S(1)}, u32[]{:S(2)}, u32[]{:S(2)}) %collective-permute-start.9) | collective-permute-done | bytes 196640 | tf_op jit(solution)/shard_map/ppermute | solution.py:174
  55.4 2.4 %collective-permute-start.8 = (bf16[2,2,192,128]{3,2,1,0:T(8,128)(2,1)S(1)}, bf16[2,2,192,128]{3,2,1,0:T(8,128)(2,1)S(1)}, u32[]{:S(2)}, u32[]{:S(2)}) collective-permute-start(bf16[2,2,192,128]{3,2,1,0:T(8,128)(2,1)S(1)} %get-tuple-element.49.own), channel_id=1, source_target_pairs={{0,8},{1,9},{2,10},{3,11},{4,12},{5,13},{6,14},{7,15},{8,0},{9,1},... | collective-permute-start | bytes 589832 | tf_op jit(solution)/shard_map/ppermute | solution.py:174
  57.9 2.3 %collective-permute-start.6 = (bf16[2,2,192,128]{3,2,1,0:T(8,128)(2,1)S(1)}, bf16[2,2,192,128]{3,2,1,0:T(8,128)(2,1)S(1)}, u32[]{:S(2)}, u32[]{:S(2)}) collective-permute-start(bf16[2,2,192,128]{3,2,1,0:T(8,128)(2,1)S(1)} %get-tuple-element.45.own), channel_id=1, source_target_pairs={{0,8},{1,9},{2,10},{3,11},{4,12},{5,13},{6,14},{7,15},{8,0},{9,1},... | collective-permute-start | bytes 589832 | tf_op jit(solution)/shard_map/ppermute | solution.py:174
  60.2 3.9 %terms.10 = (bf16[2,192,128]{2,1,0:T(8,128)(2,1)S(1)}, bf16[2,192,128]{2,1,0:T(8,128)(2,1)S(1)}, bf16[2,2,192,128]{3,2,1,0:T(8,128)(2,1)S(1)}, bf16[2,2,192,128]...) custom-call(s32[12]{0:T(128)S(1)} %iota.23.order, bf16[2,2,192,128]{3,2,1,0:T(8,128)(2,1)S(1)} %get-tuple-element.51.own, ...), custom_call_target="tpu_custom_call" | custom-call | flops 566231040 | bytes 1769472 | tf_op jit(solution)/shard_map/terms/pallas_call | solution.py:116
  66.0 3.9 %terms.11 = (bf16[2,192,128]{2,1,0:T(8,128)(2,1)S(1)}, bf16[2,192,128]{2,1,0:T(8,128)(2,1)S(1)}, bf16[2,2,192,128]{3,2,1,0:T(8,128)(2,1)S(1)}, bf16[2,2,192,128]...) custom-call(s32[12]{0:T(128)S(1)} %iota.24.order, bf16[2,2,192,128]{3,2,1,0:T(8,128)(2,1)S(1)} %get-tuple-element.53.own, ...), custom_call_target="tpu_custom_call" | custom-call | flops 566231040 | bytes 1769472 | tf_op jit(solution)/shard_map/terms/pallas_call | solution.py:116
  73.0 3.9 %terms.9 = (bf16[2,192,128]{2,1,0:T(8,128)(2,1)S(1)}, bf16[2,192,128]{2,1,0:T(8,128)(2,1)S(1)}, bf16[2,2,192,128]{3,2,1,0:T(8,128)(2,1)S(1)}, bf16[2,2,192,128]{...) custom-call(s32[12]{0:T(128)S(1)} %iota.22.order, bf16[2,2,192,128]{3,2,1,0:T(8,128)(2,1)S(1)} %get-tuple-element.49.own, ...), custom_call_target="tpu_custom_call" | custom-call | flops 566231040 | bytes 1769472 | tf_op jit(solution)/shard_map/terms/pallas_call | solution.py:116
  78.1 3.8 %terms.8 = (bf16[2,192,128]{2,1,0:T(8,128)(2,1)S(1)}, bf16[2,192,128]{2,1,0:T(8,128)(2,1)S(1)}, bf16[2,2,192,128]{3,2,1,0:T(8,128)(2,1)S(1)}, bf16[2,2,192,128]{...) custom-call(s32[12]{0:T(128)S(1)} %iota.21.order, bf16[2,2,192,128]{3,2,1,0:T(8,128)(2,1)S(1)} %get-tuple-element.47.own, ...), custom_call_target="tpu_custom_call" | custom-call | flops 566231040 | bytes 1769472 | tf_op jit(solution)/shard_map/terms/pallas_call | solution.py:116
  83.2 3.6 %collective-permute-done.other = bf16[2,2,192,128]{3,2,1,0:T(8,128)(2,1)S(1)} collective-permute-done((bf16[2,2,192,128]{3,2,1,0:T(8,128)(2,1)S(1)}, bf16[2,2,192,128]{3,2,1,0:T(8,128)(2,1)S(1)}, u32[]{:S(2)}, u32[]{:S(2)}) %collective-permute-start) | collective-permute-done | bytes 196640 | tf_op jit(solution)/shard_map/ppermute | solution.py:174
  86.8 3.9 %terms.7 = (bf16[2,192,128]{2,1,0:T(8,128)(2,1)S(1)}, bf16[2,192,128]{2,1,0:T(8,128)(2,1)S(1)}, bf16[2,2,192,128]{3,2,1,0:T(8,128)(2,1)S(1)}, bf16[2,2,192,128]{...) custom-call(s32[12]{0:T(128)S(1)} %iota.20.order, bf16[2,2,192,128]{3,2,1,0:T(8,128)(2,1)S(1)} %get-tuple-element.45.own, ...), custom_call_target="tpu_custom_call" | custom-call | flops 566231040 | bytes 1769472 | tf_op jit(solution)/shard_map/terms/pallas_call | solution.py:116
  90.7 3.9 %terms.6 = (bf16[2,192,128]{2,1,0:T(8,128)(2,1)S(1)}, bf16[2,192,128]{2,1,0:T(8,128)(2,1)S(1)}, bf16[2,2,192,128]{3,2,1,0:T(8,128)(2,1)S(1)}, bf16[2,2,192,128]{...) custom-call(s32[12]{0:T(128)S(1)} %iota.18.order, bf16[2,2,192,128]{3,2,1,0:T(8,128)(2,1)S(1)} %get-tuple-element.41.own, ...), custom_call_target="tpu_custom_call" | custom-call | flops 566231040 | bytes 1769472 | tf_op jit(solution)/shard_map/terms/pallas_call | solution.py:116
  94.6 2.4 %collective-permute-start.13 = (bf16[2,192,128]{2,1,0:T(8,128)(2,1)S(1)}, bf16[2,192,128]{2,1,0:T(8,128)(2,1)S(1)}, u32[]{:S(2)}, u32[]{:S(2)}) collective-permute-start(bf16[2,192,128]{2,1,0:T(8,128)(2,1)S(1)} %get-tuple-element.57), channel_id=1, source_target_pairs={{0,8},{1,9},{2,10},{3,11},{4,12},{5,13},{6,14},{7,15},{8,0},{9,1},... | collective-permute-start | bytes 294920 | tf_op jit(solution)/shard_map/ppermute | solution.py:174
  97.1 2.3 %collective-permute-start.11 = (bf16[2,192,128]{2,1,0:T(8,128)(2,1)S(1)}, bf16[2,192,128]{2,1,0:T(8,128)(2,1)S(1)}, u32[]{:S(2)}, u32[]{:S(2)}) collective-permute-start(bf16[2,192,128]{2,1,0:T(8,128)(2,1)S(1)} %get-tuple-element.55), channel_id=1, source_target_pairs={{0,8},{1,9},{2,10},{3,11},{4,12},{5,13},{6,14},{7,15},{8,0},{9,1},... | collective-permute-start | bytes 294920 | tf_op jit(solution)/shard_map/ppermute | solution.py:174
  99.4 5.9 %collective-permute-start.27 = (bf16[2,2,192,128]{3,2,1,0:T(8,128)(2,1)S(1)}, bf16[2,2,192,128]{3,2,1,0:T(8,128)(2,1)S(1)}, u32[]{:S(2)}, u32[]{:S(2)}) collective-permute-start(bf16[2,2,192,128]{3,2,1,0:T(8,128)(2,1)S(1)} %get-tuple-element.77), channel_id=1, source_target_pairs={{1,0},{2,1},{3,2},{4,3},{5,4},{6,5},{7,6},{9,8},{10,9},{11,10},{12... | collective-permute-start | bytes 589832 | tf_op jit(solution)/shard_map/ppermute | solution.py:174
  107.3 4.5 %collective-permute-start.20 = (bf16[2,2,192,128]{3,2,1,0:T(8,128)(2,1)S(1)}, bf16[2,2,192,128]{3,2,1,0:T(8,128)(2,1)S(1)}, u32[]{:S(2)}, u32[]{:S(2)}) collective-permute-start(bf16[2,2,192,128]{3,2,1,0:T(8,128)(2,1)S(1)} %get-tuple-element.70), channel_id=1, source_target_pairs={{0,1},{1,2},{2,3},{3,4},{4,5},{5,6},{6,7},{8,9},{9,10},{10,11},{11... | collective-permute-start | bytes 589832 | tf_op jit(solution)/shard_map/ppermute | solution.py:174
  113.8 4.5 %collective-permute-start.19 = (bf16[2,2,192,128]{3,2,1,0:T(8,128)(2,1)S(1)}, bf16[2,2,192,128]{3,2,1,0:T(8,128)(2,1)S(1)}, u32[]{:S(2)}, u32[]{:S(2)}) collective-permute-start(bf16[2,2,192,128]{3,2,1,0:T(8,128)(2,1)S(1)} %get-tuple-element.69), channel_id=1, source_target_pairs={{0,1},{1,2},{2,3},{3,4},{4,5},{5,6},{6,7},{8,9},{9,10},{10,11},{11... | collective-permute-start | bytes 589832 | tf_op jit(solution)/shard_map/ppermute | solution.py:174
  120.3 4.5 %collective-permute-start.18 = (bf16[2,2,192,128]{3,2,1,0:T(8,128)(2,1)S(1)}, bf16[2,2,192,128]{3,2,1,0:T(8,128)(2,1)S(1)}, u32[]{:S(2)}, u32[]{:S(2)}) collective-permute-start(bf16[2,2,192,128]{3,2,1,0:T(8,128)(2,1)S(1)} %get-tuple-element.68), channel_id=1, source_target_pairs={{0,1},{1,2},{2,3},{3,4},{4,5},{5,6},{6,7},{8,9},{9,10},{10,11},{11... | collective-permute-start | bytes 589832 | tf_op jit(solution)/shard_map/ppermute | solution.py:174
  126.8 4.5 %collective-permute-start.17 = (bf16[2,2,192,128]{3,2,1,0:T(8,128)(2,1)S(1)}, bf16[2,2,192,128]{3,2,1,0:T(8,128)(2,1)S(1)}, u32[]{:S(2)}, u32[]{:S(2)}) collective-permute-start(bf16[2,2,192,128]{3,2,1,0:T(8,128)(2,1)S(1)} %get-tuple-element.67), channel_id=1, source_target_pairs={{0,1},{1,2},{2,3},{3,4},{4,5},{5,6},{6,7},{8,9},{9,10},{10,11},{11... | collective-permute-start | bytes 589832 | tf_op jit(solution)/shard_map/ppermute | solution.py:174
  133.9 5.3 %collective-permute-done.23.refs_24_ = bf16[2,2,192,128]{3,2,1,0:T(8,128)(2,1)S(1)} collective-permute-done((bf16[2,2,192,128]{3,2,1,0:T(8,128)(2,1)S(1)}, bf16[2,2,192,128]{3,2,1,0:T(8,128)(2,1)S(1)}, u32[]{:S(2)}, u32[]{:S(2)}) %collective-permute-start.23) | collective-permute-done | bytes 196640 | tf_op jit(solution)/shard_map/ppermute | solution.py:174
  139.2 2.3 %finish.1 = (bf16[192,1536]{1,0:T(8,128)(2,1)}, bf16[192,1536]{1,0:T(8,128)(2,1)}, bf16[192,1536]{1,0:T(8,128)(2,1)}) custom-call(s32[12]{0:T(128)S(1)} %iota.17.order, bf16[2,192,128]{2,1,0:T(8,128)(2,1)S(1)} %get-tuple-element.44.refs_0_, bf16[2,192,128]{2,1,0:T(8,128)(2,1)S(1)} %get-tuple-element.46.refs_1_, ...), custom_call_target="tpu_custom_call" | custom-call | tf_op jit(solution)/shard_map/finish/pallas_call | solution.py:157
  (63 shorter events, 27.7 us)
Async XLA Ops:
  0.6 54.8 %collective-permute-start.2 = (bf16[192,1536]{1,0:T(8,128)(2,1)}, bf16[192,1536]{1,0:T(8,128)(2,1)S(1)}, u32[]{:S(2)}, u32[]{:S(2)}) collective-permute-start(bf16[192,1536]{1,0:T(8,128)(2,1)} %refs_0_.11), channel_id=1, source_target_pairs={{0,1},{1,2},{2,3},{3,4},{4,5},{5,6},{6,7},{8,9},{9,10},{10,11},{11... | collective-permute-start | bytes 1769480 | tf_op jit(solution)/shard_map/ppermute | solution.py:174
  4.3 53.4 %collective-permute-start.3 = (bf16[192,1536]{1,0:T(8,128)(2,1)}, bf16[192,1536]{1,0:T(8,128)(2,1)S(1)}, u32[]{:S(2)}, u32[]{:S(2)}) collective-permute-start(bf16[192,1536]{1,0:T(8,128)(2,1)} %refs_0_.11), channel_id=1, source_target_pairs={{1,0},{2,1},{3,2},{4,3},{5,4},{6,5},{7,6},{9,8},{10,9},{11,10},{12... | collective-permute-start | bytes 1769480 | tf_op jit(solution)/shard_map/ppermute | solution.py:174
  6.3 51.6 %collective-permute-start.4 = (bf16[192,1536]{1,0:T(8,128)(2,1)}, bf16[192,1536]{1,0:T(8,128)(2,1)S(1)}, u32[]{:S(2)}, u32[]{:S(2)}) collective-permute-start(bf16[192,1536]{1,0:T(8,128)(2,1)} %refs_3_.11), channel_id=1, source_target_pairs={{0,1},{1,2},{2,3},{3,4},{4,5},{5,6},{6,7},{8,9},{9,10},{10,11},{11... | collective-permute-start | bytes 1769480 | tf_op jit(solution)/shard_map/ppermute | solution.py:174
  10.8 49.3 %collective-permute-start.5 = (bf16[192,1536]{1,0:T(8,128)(2,1)}, bf16[192,1536]{1,0:T(8,128)(2,1)S(1)}, u32[]{:S(2)}, u32[]{:S(2)}) collective-permute-start(bf16[192,1536]{1,0:T(8,128)(2,1)} %refs_3_.11), channel_id=1, source_target_pairs={{1,0},{2,1},{3,2},{4,3},{5,4},{6,5},{7,6},{9,8},{10,9},{11,10},{12... | collective-permute-start | bytes 1769480 | tf_op jit(solution)/shard_map/ppermute | solution.py:174
  22.9 32.5 %collective-permute-start.9 = (bf16[2,2,192,128]{3,2,1,0:T(8,128)(2,1)S(1)}, bf16[2,2,192,128]{3,2,1,0:T(8,128)(2,1)S(1)}, u32[]{:S(2)}, u32[]{:S(2)}) collective-permute-start(bf16[2,2,192,128]{3,2,1,0:T(8,128)(2,1)S(1)} %get-tuple-element.51.own), channel_id=1, source_target_pairs={{0,8},{1,9},{2,10},{3,11},{4,12},{5,13},{6,14},{7,15},{8,0},{9,1},... | collective-permute-start | bytes 589832 | tf_op jit(solution)/shard_map/ppermute | solution.py:174
  55.4 8.7 %collective-permute-start.10 = (bf16[2,2,192,128]{3,2,1,0:T(8,128)(2,1)S(1)}, bf16[2,2,192,128]{3,2,1,0:T(8,128)(2,1)S(1)}, u32[]{:S(2)}, u32[]{:S(2)}) collective-permute-start(bf16[2,2,192,128]{3,2,1,0:T(8,128)(2,1)S(1)} %get-tuple-element.53.own), channel_id=1, source_target_pairs={{0,8},{1,9},{2,10},{3,11},{4,12},{5,13},{6,14},{7,15},{8,0},{9,1},... | collective-permute-start | bytes 589832 | tf_op jit(solution)/shard_map/ppermute | solution.py:174
  55.4 15.6 %collective-permute-start.8 = (bf16[2,2,192,128]{3,2,1,0:T(8,128)(2,1)S(1)}, bf16[2,2,192,128]{3,2,1,0:T(8,128)(2,1)S(1)}, u32[]{:S(2)}, u32[]{:S(2)}) collective-permute-start(bf16[2,2,192,128]{3,2,1,0:T(8,128)(2,1)S(1)} %get-tuple-element.49.own), channel_id=1, source_target_pairs={{0,8},{1,9},{2,10},{3,11},{4,12},{5,13},{6,14},{7,15},{8,0},{9,1},... | collective-permute-start | bytes 589832 | tf_op jit(solution)/shard_map/ppermute | solution.py:174
  57.8 19.0 %collective-permute-start.7 = (bf16[2,2,192,128]{3,2,1,0:T(8,128)(2,1)S(1)}, bf16[2,2,192,128]{3,2,1,0:T(8,128)(2,1)S(1)}, u32[]{:S(2)}, u32[]{:S(2)}) collective-permute-start(bf16[2,2,192,128]{3,2,1,0:T(8,128)(2,1)S(1)} %get-tuple-element.47.own), channel_id=1, source_target_pairs={{0,8},{1,9},{2,10},{3,11},{4,12},{5,13},{6,14},{7,15},{8,0},{9,1},... | collective-permute-start | bytes 589832 | tf_op jit(solution)/shard_map/ppermute | solution.py:174
  57.9 24.1 %collective-permute-start.6 = (bf16[2,2,192,128]{3,2,1,0:T(8,128)(2,1)S(1)}, bf16[2,2,192,128]{3,2,1,0:T(8,128)(2,1)S(1)}, u32[]{:S(2)}, u32[]{:S(2)}) collective-permute-start(bf16[2,2,192,128]{3,2,1,0:T(8,128)(2,1)S(1)} %get-tuple-element.45.own), channel_id=1, source_target_pairs={{0,8},{1,9},{2,10},{3,11},{4,12},{5,13},{6,14},{7,15},{8,0},{9,1},... | collective-permute-start | bytes 589832 | tf_op jit(solution)/shard_map/ppermute | solution.py:174
  60.2 26.7 %collective-permute-start = (bf16[2,2,192,128]{3,2,1,0:T(8,128)(2,1)S(1)}, bf16[2,2,192,128]{3,2,1,0:T(8,128)(2,1)S(1)}, u32[]{:S(2)}, u32[]{:S(2)}) collective-permute-start(bf16[2,2,192,128]{3,2,1,0:T(8,128)(2,1)S(1)} %get-tuple-element.41.own), channel_id=1, source_target_pairs={{0,8},{1,9},{2,10},{3,11},{4,12},{5,13},{6,14},{7,15},{8,0},{9,1},... | collective-permute-start | bytes 589832 | tf_op jit(solution)/shard_map/ppermute | solution.py:174
  64.1 47.7 %collective-permute-start.21 = (bf16[2,2,192,128]{3,2,1,0:T(8,128)(2,1)S(1)}, bf16[2,2,192,128]{3,2,1,0:T(8,128)(2,1)S(1)}, u32[]{:S(2)}, u32[]{:S(2)}) collective-permute-start(bf16[2,2,192,128]{3,2,1,0:T(8,128)(2,1)S(1)} %get-tuple-element.71), channel_id=1, source_target_pairs={{0,1},{1,2},{2,3},{3,4},{4,5},{5,6},{6,7},{8,9},{9,10},{10,11},{11... | collective-permute-start | bytes 589832 | tf_op jit(solution)/shard_map/ppermute | solution.py:174
  71.0 42.7 %collective-permute-start.22 = (bf16[2,2,192,128]{3,2,1,0:T(8,128)(2,1)S(1)}, bf16[2,2,192,128]{3,2,1,0:T(8,128)(2,1)S(1)}, u32[]{:S(2)}, u32[]{:S(2)}) collective-permute-start(bf16[2,2,192,128]{3,2,1,0:T(8,128)(2,1)S(1)} %get-tuple-element.72), channel_id=1, source_target_pairs={{0,1},{1,2},{2,3},{3,4},{4,5},{5,6},{6,7},{8,9},{9,10},{10,11},{11... | collective-permute-start | bytes 589832 | tf_op jit(solution)/shard_map/ppermute | solution.py:174
  76.8 17.7 %collective-permute-start.15 = (bf16[2,192,128]{2,1,0:T(8,128)(2,1)S(1)}, bf16[2,192,128]{2,1,0:T(8,128)(2,1)S(1)}, u32[]{:S(2)}, u32[]{:S(2)}) collective-permute-start(bf16[2,192,128]{2,1,0:T(8,128)(2,1)S(1)} %get-tuple-element.59), channel_id=1, source_target_pairs={{0,8},{1,9},{2,10},{3,11},{4,12},{5,13},{6,14},{7,15},{8,0},{9,1},... | collective-permute-start | bytes 294920 | tf_op jit(solution)/shard_map/ppermute | solution.py:174
  82.0 15.0 %collective-permute-start.16 = (bf16[2,192,128]{2,1,0:T(8,128)(2,1)S(1)}, bf16[2,192,128]{2,1,0:T(8,128)(2,1)S(1)}, u32[]{:S(2)}, u32[]{:S(2)}) collective-permute-start(bf16[2,192,128]{2,1,0:T(8,128)(2,1)S(1)} %get-tuple-element.60), channel_id=1, source_target_pairs={{0,8},{1,9},{2,10},{3,11},{4,12},{5,13},{6,14},{7,15},{8,0},{9,1},... | collective-permute-start | bytes 294920 | tf_op jit(solution)/shard_map/ppermute | solution.py:174
  86.8 10.3 %collective-permute-start.14 = (bf16[2,192,128]{2,1,0:T(8,128)(2,1)S(1)}, bf16[2,192,128]{2,1,0:T(8,128)(2,1)S(1)}, u32[]{:S(2)}, u32[]{:S(2)}) collective-permute-start(bf16[2,192,128]{2,1,0:T(8,128)(2,1)S(1)} %get-tuple-element.58), channel_id=1, source_target_pairs={{0,8},{1,9},{2,10},{3,11},{4,12},{5,13},{6,14},{7,15},{8,0},{9,1},... | collective-permute-start | bytes 294920 | tf_op jit(solution)/shard_map/ppermute | solution.py:174
  97.1 10.1 %collective-permute-start.11 = (bf16[2,192,128]{2,1,0:T(8,128)(2,1)S(1)}, bf16[2,192,128]{2,1,0:T(8,128)(2,1)S(1)}, u32[]{:S(2)}, u32[]{:S(2)}) collective-permute-start(bf16[2,192,128]{2,1,0:T(8,128)(2,1)S(1)} %get-tuple-element.55), channel_id=1, source_target_pairs={{0,8},{1,9},{2,10},{3,11},{4,12},{5,13},{6,14},{7,15},{8,0},{9,1},... | collective-permute-start | bytes 294920 | tf_op jit(solution)/shard_map/ppermute | solution.py:174
  99.4 18.9 %collective-permute-start.27 = (bf16[2,2,192,128]{3,2,1,0:T(8,128)(2,1)S(1)}, bf16[2,2,192,128]{3,2,1,0:T(8,128)(2,1)S(1)}, u32[]{:S(2)}, u32[]{:S(2)}) collective-permute-start(bf16[2,2,192,128]{3,2,1,0:T(8,128)(2,1)S(1)} %get-tuple-element.77), channel_id=1, source_target_pairs={{1,0},{2,1},{3,2},{4,3},{5,4},{6,5},{7,6},{9,8},{10,9},{11,10},{12... | collective-permute-start | bytes 589832 | tf_op jit(solution)/shard_map/ppermute | solution.py:174
  105.3 14.9 %collective-permute-start.28 = (bf16[2,2,192,128]{3,2,1,0:T(8,128)(2,1)S(1)}, bf16[2,2,192,128]{3,2,1,0:T(8,128)(2,1)S(1)}, u32[]{:S(2)}, u32[]{:S(2)}) collective-permute-start(bf16[2,2,192,128]{3,2,1,0:T(8,128)(2,1)S(1)} %get-tuple-element.78), channel_id=1, source_target_pairs={{1,0},{2,1},{3,2},{4,3},{5,4},{6,5},{7,6},{9,8},{10,9},{11,10},{12... | collective-permute-start | bytes 589832 | tf_op jit(solution)/shard_map/ppermute | solution.py:174
  107.3 17.5 %collective-permute-start.20 = (bf16[2,2,192,128]{3,2,1,0:T(8,128)(2,1)S(1)}, bf16[2,2,192,128]{3,2,1,0:T(8,128)(2,1)S(1)}, u32[]{:S(2)}, u32[]{:S(2)}) collective-permute-start(bf16[2,2,192,128]{3,2,1,0:T(8,128)(2,1)S(1)} %get-tuple-element.70), channel_id=1, source_target_pairs={{0,1},{1,2},{2,3},{3,4},{4,5},{5,6},{6,7},{8,9},{9,10},{10,11},{11... | collective-permute-start | bytes 589832 | tf_op jit(solution)/shard_map/ppermute | solution.py:174
  111.8 14.9 %collective-permute-start.26 = (bf16[2,2,192,128]{3,2,1,0:T(8,128)(2,1)S(1)}, bf16[2,2,192,128]{3,2,1,0:T(8,128)(2,1)S(1)}, u32[]{:S(2)}, u32[]{:S(2)}) collective-permute-start(bf16[2,2,192,128]{3,2,1,0:T(8,128)(2,1)S(1)} %get-tuple-element.76), channel_id=1, source_target_pairs={{1,0},{2,1},{3,2},{4,3},{5,4},{6,5},{7,6},{9,8},{10,9},{11,10},{12... | collective-permute-start | bytes 589832 | tf_op jit(solution)/shard_map/ppermute | solution.py:174
  113.8 17.5 %collective-permute-start.19 = (bf16[2,2,192,128]{3,2,1,0:T(8,128)(2,1)S(1)}, bf16[2,2,192,128]{3,2,1,0:T(8,128)(2,1)S(1)}, u32[]{:S(2)}, u32[]{:S(2)}) collective-permute-start(bf16[2,2,192,128]{3,2,1,0:T(8,128)(2,1)S(1)} %get-tuple-element.69), channel_id=1, source_target_pairs={{0,1},{1,2},{2,3},{3,4},{4,5},{5,6},{6,7},{8,9},{9,10},{10,11},{11... | collective-permute-start | bytes 589832 | tf_op jit(solution)/shard_map/ppermute | solution.py:174
  118.3 14.9 %collective-permute-start.25 = (bf16[2,2,192,128]{3,2,1,0:T(8,128)(2,1)S(1)}, bf16[2,2,192,128]{3,2,1,0:T(8,128)(2,1)S(1)}, u32[]{:S(2)}, u32[]{:S(2)}) collective-permute-start(bf16[2,2,192,128]{3,2,1,0:T(8,128)(2,1)S(1)} %get-tuple-element.75), channel_id=1, source_target_pairs={{1,0},{2,1},{3,2},{4,3},{5,4},{6,5},{7,6},{9,8},{10,9},{11,10},{12... | collective-permute-start | bytes 589832 | tf_op jit(solution)/shard_map/ppermute | solution.py:174
  120.3 13.0 %collective-permute-start.18 = (bf16[2,2,192,128]{3,2,1,0:T(8,128)(2,1)S(1)}, bf16[2,2,192,128]{3,2,1,0:T(8,128)(2,1)S(1)}, u32[]{:S(2)}, u32[]{:S(2)}) collective-permute-start(bf16[2,2,192,128]{3,2,1,0:T(8,128)(2,1)S(1)} %get-tuple-element.68), channel_id=1, source_target_pairs={{0,1},{1,2},{2,3},{3,4},{4,5},{5,6},{6,7},{8,9},{9,10},{10,11},{11... | collective-permute-start | bytes 589832 | tf_op jit(solution)/shard_map/ppermute | solution.py:174
  124.8 8.5 %collective-permute-start.24 = (bf16[2,2,192,128]{3,2,1,0:T(8,128)(2,1)S(1)}, bf16[2,2,192,128]{3,2,1,0:T(8,128)(2,1)S(1)}, u32[]{:S(2)}, u32[]{:S(2)}) collective-permute-start(bf16[2,2,192,128]{3,2,1,0:T(8,128)(2,1)S(1)} %get-tuple-element.74), channel_id=1, source_target_pairs={{1,0},{2,1},{3,2},{4,3},{5,4},{6,5},{7,6},{9,8},{10,9},{11,10},{12... | collective-permute-start | bytes 589832 | tf_op jit(solution)/shard_map/ppermute | solution.py:174
  (11 other events, 121.7 us)
